TPU v7x, 128 devices: a whole 4x4x4 slice. The times are simulated.
128 devices in a mesh: pose: 16 (over y_hi, z, core), text: 8 (over y_lo, x).
Axes of the slice: x: 4, y: 4 (y_hi: 2, y_lo: 2; y = y_hi * 2 + y_lo), z: 4, core: 2. Of those that a mesh axis runs over, the one named last changes fastest.
Arguments:
- pose_emb: float32 [16384, 768], P(('pose', 'text')), may hold values from -100 to 100
- text_emb: float32 [16384, 768], P(('pose', 'text')), may hold values from -6 to 6
- positive: int32 [16384], P(('pose', 'text')), may hold values from 0 to 16383, each once
Outputs:
- loss: float32 [], replicated
- pose_grad: float32 [16384, 768], P(('pose', 'text'))
- text_grad: float32 [16384, 768], P(('pose', 'text'))
All inputs are finite; a program needn't handle non-finite values.
Results may differ from a plain program's by a relative error of at most 0.0003.
Values sent between devices are 32-bit elements; how exact they have to be, the bound alone decides.
A program may use at most 64 MiB of HBM per device.

v0:
```python
import math

import jax
import jax.numpy as jnp
from jax import lax
from jax.sharding import PartitionSpec as P


def combined_all(part, axis, combine):
    gathered = jax.tree.map(lambda a: lax.all_gather(a, axis), part)

    def take(source):
        return jax.tree.map(lambda a: lax.dynamic_index_in_dim(a, source, 0, False), gathered)

    return lax.fori_loop(
        1, lax.axis_size(axis), lambda source, state: combine(state, take(source)), take(0)
    )


def combine_stats(first, second):
    top = jnp.maximum(first[0], second[0])
    total = first[1] * jnp.exp(first[0] - top) + second[1] * jnp.exp(second[0] - top)
    return (top, total)


def logit_block(rows, cols, scale):
    return scale * jnp.dot(
        rows, cols.T, precision=lax.Precision.HIGHEST, preferred_element_type=jnp.float32
    )


def slope_block(logits, row_ids, col_ids, row_lse, col_lse):
    hit = (row_ids[:, None] == col_ids[None, :]).astype(jnp.float32)
    return 0.5 * (jnp.exp(logits - row_lse[:, None]) + jnp.exp(logits - col_lse[None, :])) - hit


def block_stats(pose_blk, pose_ids, text_blk, col_ids, scale):
    rows_all = pose_blk.shape[0]
    step = math.gcd(rows_all, 256)

    def block_one(carry, k):
        col_top, col_sum, matched = carry
        start = k * step
        part = lax.dynamic_slice_in_dim(pose_blk, start, step, 0)
        row_ids = lax.dynamic_slice_in_dim(pose_ids, start, step, 0)
        logits = logit_block(part, text_blk, scale)
        row_top = jnp.max(logits, axis=1)
        row_sum = jnp.sum(jnp.exp(logits - row_top[:, None]), axis=1)
        new_top = jnp.maximum(col_top, jnp.max(logits, axis=0))
        new_sum = col_sum * jnp.exp(col_top - new_top) + jnp.sum(
            jnp.exp(logits - new_top[None, :]), axis=0
        )
        hit = row_ids[:, None] == col_ids[None, :]
        matched = matched + jnp.sum(jnp.where(hit, logits, jnp.float32(0.0)))
        return ((new_top, new_sum, matched), (row_top, row_sum))

    cols_all = text_blk.shape[0]
    init = (
        jnp.full((cols_all,), -jnp.inf, jnp.float32),
        jnp.zeros((cols_all,), jnp.float32),
        jnp.zeros((), jnp.float32),
    )
    (col_top, col_sum, matched), (row_top, row_sum) = lax.scan(
        block_one, init, jnp.arange(rows_all // step, dtype=jnp.int32)
    )
    return (row_top.reshape(rows_all), row_sum.reshape(rows_all), col_top, col_sum, matched)


def gradient_pass(pose_blk, pose_ids, text_blk, col_ids, row_lse, col_lse, scale):
    rows_all = pose_blk.shape[0]
    width = pose_blk.shape[1]
    step = math.gcd(rows_all, 256)

    def gradient_one(acc, k):
        begin = k * step
        part = lax.dynamic_slice_in_dim(pose_blk, begin, step, 0)
        row_ids = lax.dynamic_slice_in_dim(pose_ids, begin, step, 0)
        lse_part = lax.dynamic_slice_in_dim(row_lse, begin, step, 0)
        slope = slope_block(logit_block(part, text_blk, scale), row_ids, col_ids, lse_part, col_lse)
        pose_piece = scale * jnp.dot(
            slope, text_blk, precision=lax.Precision.HIGHEST, preferred_element_type=jnp.float32
        )
        acc = acc + scale * lax.dot_general(
            slope,
            part,
            (((0,), (0,)), ((), ())),
            precision=lax.Precision.HIGHEST,
            preferred_element_type=jnp.float32,
        )
        return (acc, pose_piece)

    text_part, pose_pieces = lax.scan(
        gradient_one,
        jnp.zeros((text_blk.shape[0], width), jnp.float32),
        jnp.arange(rows_all // step, dtype=jnp.int32),
    )
    return (pose_pieces.reshape(rows_all, width), text_part)


def per_device(pose_emb, text_emb, positive):
    local = text_emb.shape[0]
    width = text_emb.shape[1]
    scale = 2.0 / math.sqrt(width)
    across = lax.axis_size("text")
    total = local * lax.axis_size("pose") * across
    text_at = lax.axis_index("text")
    id_floats = positive.astype(jnp.float32)
    pose_blk, id_vals = (
        lax.all_gather(pose_emb, "text", axis=0, tiled=True),
        lax.all_gather(id_floats, "text", axis=0, tiled=True),
    )
    text_blk = lax.all_gather(text_emb, "pose", axis=0, tiled=True)
    slot = jnp.arange(text_blk.shape[0], dtype=jnp.int32)
    col_ids = (slot // local * across + text_at) * local + slot % local
    pose_ids = id_vals.astype(jnp.int32)
    row_top, row_sum, col_top, col_sum, matched = block_stats(
        pose_blk, pose_ids, text_blk, col_ids, scale
    )
    row_top, row_sum = combined_all((row_top, row_sum), "text", combine_stats)
    col_top, col_sum = combined_all((col_top, col_sum), "pose", combine_stats)
    row_lse = row_top + jnp.log(row_sum)
    col_lse = col_top + jnp.log(col_sum)
    share = (
        0.5 * (jnp.sum(row_lse) / lax.axis_size("text") + jnp.sum(col_lse) / lax.axis_size("pose"))
        - matched
    )
    pose_part, text_part = gradient_pass(
        pose_blk, pose_ids, text_blk, col_ids, row_lse, col_lse, scale
    )
    pose_grad = lax.psum_scatter(pose_part, "text", scatter_dimension=0, tiled=True)
    text_grad = lax.psum_scatter(text_part, "pose", scatter_dimension=0, tiled=True)
    loss = lax.psum(share, ("pose", "text")) / total
    return (loss, pose_grad, text_grad)


def solution(mesh):
    return jax.shard_map(
        per_device,
        mesh=mesh,
        in_specs=(P(("pose", "text"), None), P(("pose", "text"), None), P(("pose", "text"))),
        out_specs=(P(), P(("pose", "text"), None), P(("pose", "text"), None)),
        check_vma=False,
    )
```

profile of v0, /device:TPU:1, one launch (start us, length us, event | category | flops | bytes accessed | tf_op | source)
XLA Modules:
  0.0 525.3 jit_solution(800383523673489793)
XLA Ops:
  9.4 15.8 %all-gather.2 = f32[8,1,128]{2,1,0:T(1,128)S(1)} all-gather(f32[1,1,128]{2,1,0:T(1,128)S(1)} %convert_bitcast_fusion), channel_id=1, replica_groups=mesh['pose'=16,'text'=8] {'text'}, dimensions={0}, use_global_device_ids=true | all-gather | bytes 4608 | tf_op jit(solution)/shard_map/all_gather | solution.py:110
  25.2 29.2 %all-gather.8.cloned.1.call-done = f32[1024,768]{1,0:T(8,128)} async-done(((f32[128,768]{1,0:T(8,128)}), f32[1024,768]{1,0:T(8,128)}) %all-gather.8.cloned.1.call-update) | async-done | bytes 3145744 | tf_op jit(solution)/shard_map/all_gather | solution.py:109
  54.4 69.6 %all-gather.10.cloned.1.call-done = f32[2048,768]{1,0:T(8,128)} async-done(((f32[128,768]{1,0:T(8,128)}), f32[2048,768]{1,0:T(8,128)}) %all-gather.10.cloned.1.call-update) | async-done | bytes 6291472 | tf_op jit(solution)/shard_map/all_gather | solution.py:112
  124.0 46.0 %while.68 = (s32[]{:T(128)}, f32[2048]{0:T(1024)S(1)}, f32[2048]{0:T(1024)S(1)}, f32[]{:T(128)}, f32[4,256]{1,0:T(4,128)S(1)}, /*index=5*/f32[4,256]{1,0:T(4,128...) while((s32[]{:T(128)}, f32[2048]{0:T(1024)S(1)}, ...), condition=%wide.region_6.7_spmd.clone, body=%wide.region_0.6_spmd.clone.sunk | while | flops 4837123584 | bytes 11405566 | solution.py:63
  125.2 7.9 %fusion.56 = (f32[256]{0:T(256)S(1)}, f32[2048]{0:T(1024)S(1)}, f32[256,2048]{1,0:T(8,128)S(1)}) fusion(f32[2048,768]{1,0:T(8,128)} %get-tuple-element.805, f32[1024,768]{1,0:T(8,128)} %get-tuple-element.804, s32[]{:T(128)S(6)} %select_n.111), kind=kOutput, calls=%fused_computation.62.clone.1 | convolution fusion | flops 4833409024 | bytes 9184260 | tf_op jit(solution)/shard_map/while/body/eval_jaxpr/dot_general | solution.py:27
  136.7 8.0 %fusion.56 = (f32[256]{0:T(256)S(1)}, f32[2048]{0:T(1024)S(1)}, f32[256,2048]{1,0:T(8,128)S(1)}) fusion(f32[2048,768]{1,0:T(8,128)} %get-tuple-element.805, f32[1024,768]{1,0:T(8,128)} %get-tuple-element.804, s32[]{:T(128)S(6)} %select_n.111), kind=kOutput, calls=%fused_computation.62.clone.1 | convolution fusion | flops 4833409024 | bytes 9184260 | tf_op jit(solution)/shard_map/while/body/eval_jaxpr/dot_general | solution.py:27
  144.7 1.6 exponential_reduce_fusion.3
  148.2 8.0 %fusion.56 = (f32[256]{0:T(256)S(1)}, f32[2048]{0:T(1024)S(1)}, f32[256,2048]{1,0:T(8,128)S(1)}) fusion(f32[2048,768]{1,0:T(8,128)} %get-tuple-element.805, f32[1024,768]{1,0:T(8,128)} %get-tuple-element.804, s32[]{:T(128)S(6)} %select_n.111), kind=kOutput, calls=%fused_computation.62.clone.1 | convolution fusion | flops 4833409024 | bytes 9184260 | tf_op jit(solution)/shard_map/while/body/eval_jaxpr/dot_general | solution.py:27
  159.7 8.0 %fusion.56 = (f32[256]{0:T(256)S(1)}, f32[2048]{0:T(1024)S(1)}, f32[256,2048]{1,0:T(8,128)S(1)}) fusion(f32[2048,768]{1,0:T(8,128)} %get-tuple-element.805, f32[1024,768]{1,0:T(8,128)} %get-tuple-element.804, s32[]{:T(128)S(6)} %select_n.111), kind=kOutput, calls=%fused_computation.62.clone.1 | convolution fusion | flops 4833409024 | bytes 9184260 | tf_op jit(solution)/shard_map/while/body/eval_jaxpr/dot_general | solution.py:27
  170.0 21.7 %all-gather.3 = f32[8,1,1024]{2,1,0:T(1,128)S(1)} all-gather(f32[1,1,1024]{2,1,0:T(1,128)S(1)} %reshape.30), channel_id=1, replica_groups=mesh['pose'=16,'text'=8] {'text'}, dimensions={0}, use_global_device_ids=true | all-gather | bytes 36864 | tf_op jit(solution)/shard_map/all_gather | solution.py:10
  191.8 21.7 %all-gather.4 = f32[8,1,1024]{2,1,0:T(1,128)S(1)} all-gather(f32[1,1,1024]{2,1,0:T(1,128)S(1)} %reshape.32), channel_id=1, replica_groups=mesh['pose'=16,'text'=8] {'text'}, dimensions={0}, use_global_device_ids=true | all-gather | bytes 36864 | tf_op jit(solution)/shard_map/all_gather | solution.py:10
  213.5 33.7 %all-gather = f32[32768]{0:T(1024)S(1)} all-gather(f32[2048]{0:T(1024)S(1)} %get-tuple-element.387), channel_id=2, replica_groups=mesh['pose'=16,'text'=8] {'pose'}, dimensions={0}, use_global_device_ids=true | all-gather | bytes 139264 | tf_op jit(solution)/shard_map/all_gather | solution.py:10
  247.2 19.7 %all-gather.1 = f32[32768]{0:T(1024)S(1)} all-gather(f32[2048]{0:T(1024)S(1)} %get-tuple-element.388), channel_id=3, replica_groups=mesh['pose'=16,'text'=8] {'pose'}, dimensions={0}, use_global_device_ids=true | all-gather | bytes 139264 | tf_op jit(solution)/shard_map/all_gather | solution.py:10
  269.6 110.3 %while.69 = (s32[]{:T(128)}, f32[2048,768]{1,0:T(8,128)}, f32[4,256,768]{2,1,0:T(8,128)}, s32[4]{0:T(128)S(1)}, f32[1024,768]{1,0:T(8,128)}, /*index=5*/f32[2048...) while((s32[]{:T(128)}, f32[2048,768]{1,0:T(8,128)}, ...), condition=%wide.region_15.16_spmd.clone, body=%wide.region_14.15_spmd.clone.sunk | while | flops 14504656896 | bytes 109345080 | solution.py:92
  271.0 8.5 %convert_subtract_fusion.2 = f32[256,2048]{1,0:T(8,128)S(1)} fusion(f32[2048,768]{1,0:T(8,128)} %get-tuple-element.893, s32[2048]{0:T(1024)S(1)} %fusion.65, f32[2048]{0:T(1024)S(1)} %get-tuple-element.895, f32[256]{0:T(256)S(1)} %dynamic_slice.117, s32[256]{0:T(256)S(1)} %dynamic_slice.118, f32[1024,768]{1,0:T(8,128)} %get-tuple-element.892, ...), kind=kOutput, calls=%fused_computation.34.clone.1 | convolution fusion | flops 4836032512 | bytes 9193476 | tf_op jit(solution)/shard_map/while/body/eval_jaxpr/dot_general | solution.py:27
  279.5 6.4 %fusion.66 = f32[4,256,768]{2,1,0:T(8,128)} fusion(f32[4,256,768]{2,1,0:T(8,128)} %get-tuple-element.876, s32[]{:T(128)S(6)} %copy.56, f32[256,2048]{1,0:T(8,128)S(1)} %convert_subtract_fusion.2, f32[2048,768]{1,0:T(8,128)S(1)} %copy-done), kind=kOutput, calls=%fused_computation.37.clone.1 | convolution fusion | flops 4832034816 | bytes 9175044 | tf_op jit(solution)/shard_map/while/body/eval_jaxpr/dot_general | solution.py:80
  285.9 8.6 %select_add_fusion.2 = f32[2048,768]{1,0:T(8,128)S(1)} fusion(f32[2048,768]{1,0:T(8,128)S(1)} %copy-done.1, f32[256,2048]{1,0:T(8,128)S(1)} %convert_subtract_fusion.2, pred[]{:T(512)S(6)} %compare.10, f32[1024,768]{1,0:T(8,128)} %get-tuple-element.892, s32[]{:T(128)S(6)} %select_n.114), kind=kOutput, calls=%fused_computation.32.clone.1 | convolution fusion | flops 4836556800 | bytes 15466501 | tf_op jit(solution)/shard_map/while/body/eval_jaxpr/dot_general | solution.py:83
  294.5 2.6 copy-done.2
  298.5 8.5 %convert_subtract_fusion.2 = f32[256,2048]{1,0:T(8,128)S(1)} fusion(f32[2048,768]{1,0:T(8,128)} %get-tuple-element.893, s32[2048]{0:T(1024)S(1)} %fusion.65, f32[2048]{0:T(1024)S(1)} %get-tuple-element.895, f32[256]{0:T(256)S(1)} %dynamic_slice.117, s32[256]{0:T(256)S(1)} %dynamic_slice.118, f32[1024,768]{1,0:T(8,128)} %get-tuple-element.892, ...), kind=kOutput, calls=%fused_computation.34.clone.1 | convolution fusion | flops 4836032512 | bytes 9193476 | tf_op jit(solution)/shard_map/while/body/eval_jaxpr/dot_general | solution.py:27
  307.0 6.4 %fusion.66 = f32[4,256,768]{2,1,0:T(8,128)} fusion(f32[4,256,768]{2,1,0:T(8,128)} %get-tuple-element.876, s32[]{:T(128)S(6)} %copy.56, f32[256,2048]{1,0:T(8,128)S(1)} %convert_subtract_fusion.2, f32[2048,768]{1,0:T(8,128)S(1)} %copy-done), kind=kOutput, calls=%fused_computation.37.clone.1 | convolution fusion | flops 4832034816 | bytes 9175044 | tf_op jit(solution)/shard_map/while/body/eval_jaxpr/dot_general | solution.py:80
  313.4 8.6 %select_add_fusion.2 = f32[2048,768]{1,0:T(8,128)S(1)} fusion(f32[2048,768]{1,0:T(8,128)S(1)} %copy-done.1, f32[256,2048]{1,0:T(8,128)S(1)} %convert_subtract_fusion.2, pred[]{:T(512)S(6)} %compare.10, f32[1024,768]{1,0:T(8,128)} %get-tuple-element.892, s32[]{:T(128)S(6)} %select_n.114), kind=kOutput, calls=%fused_computation.32.clone.1 | convolution fusion | flops 4836556800 | bytes 15466501 | tf_op jit(solution)/shard_map/while/body/eval_jaxpr/dot_general | solution.py:83
  322.1 2.6 copy-done.2
  326.1 8.5 %convert_subtract_fusion.2 = f32[256,2048]{1,0:T(8,128)S(1)} fusion(f32[2048,768]{1,0:T(8,128)} %get-tuple-element.893, s32[2048]{0:T(1024)S(1)} %fusion.65, f32[2048]{0:T(1024)S(1)} %get-tuple-element.895, f32[256]{0:T(256)S(1)} %dynamic_slice.117, s32[256]{0:T(256)S(1)} %dynamic_slice.118, f32[1024,768]{1,0:T(8,128)} %get-tuple-element.892, ...), kind=kOutput, calls=%fused_computation.34.clone.1 | convolution fusion | flops 4836032512 | bytes 9193476 | tf_op jit(solution)/shard_map/while/body/eval_jaxpr/dot_general | solution.py:27
  334.6 6.4 %fusion.66 = f32[4,256,768]{2,1,0:T(8,128)} fusion(f32[4,256,768]{2,1,0:T(8,128)} %get-tuple-element.876, s32[]{:T(128)S(6)} %copy.56, f32[256,2048]{1,0:T(8,128)S(1)} %convert_subtract_fusion.2, f32[2048,768]{1,0:T(8,128)S(1)} %copy-done), kind=kOutput, calls=%fused_computation.37.clone.1 | convolution fusion | flops 4832034816 | bytes 9175044 | tf_op jit(solution)/shard_map/while/body/eval_jaxpr/dot_general | solution.py:80
  341.0 8.6 %select_add_fusion.2 = f32[2048,768]{1,0:T(8,128)S(1)} fusion(f32[2048,768]{1,0:T(8,128)S(1)} %copy-done.1, f32[256,2048]{1,0:T(8,128)S(1)} %convert_subtract_fusion.2, pred[]{:T(512)S(6)} %compare.10, f32[1024,768]{1,0:T(8,128)} %get-tuple-element.892, s32[]{:T(128)S(6)} %select_n.114), kind=kOutput, calls=%fused_computation.32.clone.1 | convolution fusion | flops 4836556800 | bytes 15466501 | tf_op jit(solution)/shard_map/while/body/eval_jaxpr/dot_general | solution.py:83
  349.6 2.6 copy-done.2
  353.7 8.5 %convert_subtract_fusion.2 = f32[256,2048]{1,0:T(8,128)S(1)} fusion(f32[2048,768]{1,0:T(8,128)} %get-tuple-element.893, s32[2048]{0:T(1024)S(1)} %fusion.65, f32[2048]{0:T(1024)S(1)} %get-tuple-element.895, f32[256]{0:T(256)S(1)} %dynamic_slice.117, s32[256]{0:T(256)S(1)} %dynamic_slice.118, f32[1024,768]{1,0:T(8,128)} %get-tuple-element.892, ...), kind=kOutput, calls=%fused_computation.34.clone.1 | convolution fusion | flops 4836032512 | bytes 9193476 | tf_op jit(solution)/shard_map/while/body/eval_jaxpr/dot_general | solution.py:27
  362.2 6.5 %fusion.66 = f32[4,256,768]{2,1,0:T(8,128)} fusion(f32[4,256,768]{2,1,0:T(8,128)} %get-tuple-element.876, s32[]{:T(128)S(6)} %copy.56, f32[256,2048]{1,0:T(8,128)S(1)} %convert_subtract_fusion.2, f32[2048,768]{1,0:T(8,128)S(1)} %copy-done), kind=kOutput, calls=%fused_computation.37.clone.1 | convolution fusion | flops 4832034816 | bytes 9175044 | tf_op jit(solution)/shard_map/while/body/eval_jaxpr/dot_general | solution.py:80
  368.6 8.6 %select_add_fusion.2 = f32[2048,768]{1,0:T(8,128)S(1)} fusion(f32[2048,768]{1,0:T(8,128)S(1)} %copy-done.1, f32[256,2048]{1,0:T(8,128)S(1)} %convert_subtract_fusion.2, pred[]{:T(512)S(6)} %compare.10, f32[1024,768]{1,0:T(8,128)} %get-tuple-element.892, s32[]{:T(128)S(6)} %select_n.114), kind=kOutput, calls=%fused_computation.32.clone.1 | convolution fusion | flops 4836556800 | bytes 15466501 | tf_op jit(solution)/shard_map/while/body/eval_jaxpr/dot_general | solution.py:83
  377.2 2.6 copy-done.2
  381.8 71.1 %psum.7 = f32[]{:T(128)} all-reduce(f32[]{:T(128)S(6)} %sub.88), channel_id=1, replica_groups=mesh['pose'=16,'text'=8] {'pose','text'}, use_global_device_ids=true, to_apply=%region_13.14 | all-reduce | flops 1 | bytes 8 | tf_op jit(solution)/shard_map/psum | solution.py:132
  453.5 64.1 %reduce-scatter.5.cloned.1.call-done = f32[128,768]{1,0:T(8,128)} async-done(((f32[2048,768]{1,0:T(8,128)}), f32[128,768]{1,0:T(8,128)}) %reduce-scatter.5.cloned.1.call-update) | async-done | bytes 393232 | tf_op jit(solution)/shard_map/reduce_scatter | solution.py:131
  (148 shorter events, 17.1 us)
Async XLA Ops:
  7.2 47.2 %all-gather.8.cloned.1.call-start = ((), (), s32[]{:S(2)}) async-start(), calls=%async_computation.2 | async-start | bytes 3538944 | tf_op jit(solution)/shard_map/all_gather | solution.py:109
  7.9 116.1 %all-gather.10.cloned.1.call-start = ((), (), s32[]{:S(2)}) async-start(), calls=%async_computation.3 | async-start | bytes 6684672 | tf_op jit(solution)/shard_map/all_gather | solution.py:112
  8.6 444.8 %reduce-scatter.3.cloned.1.call-start = ((), (), s32[]{:S(2)}) async-start(), calls=%async_computation.4 | async-start | bytes 3538944 | tf_op jit(solution)/shard_map/reduce_scatter | solution.py:130
  271.0 8.5 %copy-start = (f32[2048,768]{1,0:T(8,128)S(1)}, f32[2048,768]{1,0:T(8,128)}, u32[]{:S(2)}) copy-start(f32[2048,768]{1,0:T(8,128)} %get-tuple-element.893) | copy-start | bytes 18874372 | tf_op jit(solution)/shard_map/while
  279.4 6.4 %copy-start.1 = (f32[2048,768]{1,0:T(8,128)S(1)}, f32[2048,768]{1,0:T(8,128)}, u32[]{:S(2)}) copy-start(f32[2048,768]{1,0:T(8,128)} %get-tuple-element.875) | copy-start | bytes 18874372 | tf_op jit(solution)/shard_map/while
  294.5 2.7 copy-start.2
  298.5 8.5 %copy-start = (f32[2048,768]{1,0:T(8,128)S(1)}, f32[2048,768]{1,0:T(8,128)}, u32[]{:S(2)}) copy-start(f32[2048,768]{1,0:T(8,128)} %get-tuple-element.893) | copy-start | bytes 18874372 | tf_op jit(solution)/shard_map/while
  307.0 6.4 %copy-start.1 = (f32[2048,768]{1,0:T(8,128)S(1)}, f32[2048,768]{1,0:T(8,128)}, u32[]{:S(2)}) copy-start(f32[2048,768]{1,0:T(8,128)} %get-tuple-element.875) | copy-start | bytes 18874372 | tf_op jit(solution)/shard_map/while
  322.1 2.7 copy-start.2
  326.1 8.5 %copy-start = (f32[2048,768]{1,0:T(8,128)S(1)}, f32[2048,768]{1,0:T(8,128)}, u32[]{:S(2)}) copy-start(f32[2048,768]{1,0:T(8,128)} %get-tuple-element.893) | copy-start | bytes 18874372 | tf_op jit(solution)/shard_map/while
  334.6 6.4 %copy-start.1 = (f32[2048,768]{1,0:T(8,128)S(1)}, f32[2048,768]{1,0:T(8,128)}, u32[]{:S(2)}) copy-start(f32[2048,768]{1,0:T(8,128)} %get-tuple-element.875) | copy-start | bytes 18874372 | tf_op jit(solution)/shard_map/while
  349.6 2.7 copy-start.2
  353.7 8.5 %copy-start = (f32[2048,768]{1,0:T(8,128)S(1)}, f32[2048,768]{1,0:T(8,128)}, u32[]{:S(2)}) copy-start(f32[2048,768]{1,0:T(8,128)} %get-tuple-element.893) | copy-start | bytes 18874372 | tf_op jit(solution)/shard_map/while
  362.1 6.5 %copy-start.1 = (f32[2048,768]{1,0:T(8,128)S(1)}, f32[2048,768]{1,0:T(8,128)}, u32[]{:S(2)}) copy-start(f32[2048,768]{1,0:T(8,128)} %get-tuple-element.875) | copy-start | bytes 18874372 | tf_op jit(solution)/shard_map/while
  377.2 2.7 copy-start.2
  379.9 137.7 %reduce-scatter.5.cloned.1.call-start = ((), (), s32[]{:S(2)}) async-start(), calls=%async_computation.5 | async-start | bytes 6684672 | tf_op jit(solution)/shard_map/reduce_scatter | solution.py:131
Sparse Core Ops, SparseCore 0:
  9.6 44.7 all-gather.7
  56.9 67.0 all-gather.9
  380.0 40.8 reduce-scatter.2
  425.6 91.9 reduce-scatter.4
where the time goes:
time: 526 us; the launch traced here: 525 us
  blocking collectives  184 us (35%)
  waiting for transfers between devices  165 us (31%)
  matrix products  126 us (24%)
  local copies, waits for them, and re-layouts  16.9 us (3%)
  between operations  16.9 us (3%)
  other arithmetic  8.91 us (2%)
  loops' own time  8.15 us (2%)
    all_gather x4, blocking collectives, combined_all(): gathered = jax.tree.map(lambda a: lax.all_gather(a, axis), part)  96.8 us
    psum x1, blocking collectives, per_device(): loss = lax.psum(share, ('pose', 'text')) / total  71.1 us
    all_gather x1, waiting for transfers between devices, per_device(): text_blk = lax.all_gather(text_emb, 'pose', axis=0, tiled=True)  69.6 us
    dot_general x8, matrix products, logit_block(): jnp.dot(rows, cols.T, precision=lax.Precision.HIGHEST, preferred_element_...  65.6 us
    reduce_scatter x1, waiting for transfers between devices, per_device(): lax.psum_scatter(text_part, 'pose', scatter_dimension=0, tiled=True)  64.1 us
    dot_general x4, matrix products, gradient_one(): lax.dot_general(slope, part, (((0,), (0,)), ((), ())), precision=lax.Prec...  34.4 us
    all_gather x1, waiting for transfers between devices, per_device(): lax.all_gather(pose_emb, 'text', axis=0, tiled=True)  29.2 us
    dot_general x4, matrix products, gradient_one(): jnp.dot(slope, text_blk, precision=lax.Precision.HIGHEST, preferred_eleme...  25.7 us
  transfers between devices with their start and end apart: 4, of which 3 were waited for; matrix products, arithmetic and copies ran while one was open for 0% of the time, Pallas kernels for 0%

commit v1 on v0

v1 whole, which is shorter than its diff:
```python
import functools
import math

import jax
import jax.numpy as jnp
from jax import lax
from jax.experimental import pallas as pl
from jax.experimental.pallas import tpu as pltpu
from jax.sharding import PartitionSpec as P

F32 = jnp.float32
BF16 = jnp.bfloat16
U = 128
H = U // 2


def split(v):
    hi = v.astype(BF16)
    return hi, (v - hi.astype(F32)).astype(BF16)


def dot_nt(a, b):
    return lax.dot_general(a, b, (((1,), (1,)), ((), ())), preferred_element_type=F32)


def dot_nn(a, b):
    return jnp.dot(a, b, preferred_element_type=F32)


def pick(k, values):
    out = values[-1]
    for i in range(len(values) - 2, -1, -1):
        out = jnp.where(k == i, values[i], out)
    return out


def loop(n, body):
    def step(i, carry):
        body(i)
        return carry

    lax.fori_loop(0, n, step, 0)


def kernel(
    scale,
    total,
    pose_ref,
    text_ref,
    pos_ref,
    loss_ref,
    pg_ref,
    tg_ref,
    xf,
    tf,
    xhl,
    xt,
    thl,
    lg,
    s_hi,
    s_lo,
    gp,
    gt,
    rp,
    rt,
    rsib,
    posbuf,
    rowst,
    colst,
    rowrec,
    colrec,
    la,
    lb,
    macc,
    ag_send,
    ag_recv,
    sib_send,
    sib_recv,
    pos_send,
    pos_recv,
    row_send,
    row_recv,
    col_send,
    col_recv,
    la_send,
    la_recv,
    lb_send,
    lb_recv,
    rs_send,
    rs_recv,
    rsib_send,
    rsib_recv,
):
    width = pose_ref.shape[1]
    pi = lax.axis_index("pose")
    ti = lax.axis_index("text")
    yhi, z, core = pi // 8, (pi // 2) % 4, pi % 2
    ylo, x = ti // 4, ti % 4

    def pabs(dy, dx):
        return (ylo + dy) % 2 * 4 + (x + dx) % 4

    def qabs(dy, dz):
        return (yhi + dy) % 2 * 4 + (z + dz) % 4

    def pose_peer(dy, dx):
        return (pi, pabs(dy, dx))

    def text_peer(dy, dz, dc=0):
        return (qabs(dy, dz) * 2 + (core + dc) % 2, (ylo + dy) % 2 * 4 + x)

    pose_peers = [(dy, dx) for dy in range(2) for dx in range(4) if (dy, dx) != (0, 0)]
    text_peers = [
        (dy, dz, dc)
        for dy in range(2)
        for dz in range(4)
        for dc in range(2)
        if (dy, dz, dc) != (0, 0, 0)
    ]

    barrier = pltpu.get_barrier_semaphore()
    for d in pose_peers:
        pl.semaphore_signal(barrier, inc=1, device_id=pose_peer(*d), device_id_type=pl.DeviceIdType.MESH)
    for d in text_peers:
        pl.semaphore_signal(barrier, inc=1, device_id=text_peer(*d), device_id_type=pl.DeviceIdType.MESH)
    me_p = pabs(0, 0)
    me_q = pi
    xf[me_p] = pose_ref[...]
    tf[me_q] = text_ref[...]
    posbuf[me_p] = jnp.broadcast_to(pos_ref[...], (8, U))
    pl.semaphore_wait(barrier, len(pose_peers) + len(text_peers))

    pending = []

    def copy(src, dst, ssem, rsem, dev):
        c = pltpu.make_async_remote_copy(
            src_ref=src,
            dst_ref=dst,
            send_sem=ssem,
            recv_sem=rsem,
            device_id=dev,
            device_id_type=pl.DeviceIdType.MESH,
        )
        c.start()
        pending.append(c)
        return c

    def await_recv(dst, rsem):
        pltpu.make_async_copy(dst, dst, rsem).wait()

    def buf(kind, dy, dd, h):
        if kind == 0:
            return xf.at[pabs(dy, dd), pl.ds(h * H, H)]
        return tf.at[qabs(dy, dd) * 2 + core, pl.ds(h * H, H)]

    def sib_buf(dy, dd, h, mine):
        c = core if mine else 1 - core
        return tf.at[qabs(dy, dd) * 2 + c, pl.ds(h * H, H)]

    def peer(kind, dy, dd):
        return pose_peer(dy, dd) if kind == 0 else text_peer(dy, dd, 0)

    send_count = [0, 0]

    def send(kind, src, h, to, arrives):
        n = send_count[kind]
        send_count[kind] += 1
        b = buf(kind, *src, h)
        copy(b, b, ag_send.at[kind, n], ag_recv.at[kind, (arrives[0] * 4 + arrives[1]) * 2 + h], peer(kind, *to))

    def got(kind, slot, h):
        await_recv(buf(kind, *slot, h), ag_recv.at[kind, (slot[0] * 4 + slot[1]) * 2 + h])
        if kind == 1:
            share(slot, h)

    def share(slot, h):
        i = (slot[0] * 4 + slot[1]) * 2 + h
        b = sib_buf(*slot, h, True)
        copy(b, b, sib_send.at[i], sib_recv.at[i], text_peer(0, 0, 1))

    def got_sib(slot):
        for h in range(2):
            i = (slot[0] * 4 + slot[1]) * 2 + h
            await_recv(sib_buf(*slot, h, False), sib_recv.at[i])

    NXT, PRV, PAR = (0, 1), (0, 3), (1, 0)
    for h in range(2):
        for kind in range(2):
            send(kind, (0, 0), h, NXT, (0, 3))
            send(kind, (0, 0), h, PRV, (0, 1))
            send(kind, (0, 0), h, PAR, (1, 0))
        share((0, 0), h)
    for n, d in enumerate(pose_peers):
        b = posbuf.at[me_p]
        copy(b, b, pos_send.at[n], pos_recv.at[(-d[0]) % 2 * 4 + (-d[1]) % 4], pose_peer(*d))

    def convert_pose(slot):
        a = pabs(*slot)
        v = xf[a]
        hi, lo = split(v)
        rows = pl.ds(pl.multiple_of(a * U, U), U)
        xhl[0, rows, :] = hi
        xhl[1, rows, :] = lo
        vt = v.T
        hi, lo = split(vt)
        xt[0, :, rows] = hi
        xt[1, :, rows] = lo

    def convert_text(slot):
        q = qabs(*slot)
        for c in range(2):
            hi, lo = split(tf[q * 2 + c])
            rows = pl.ds(pl.multiple_of((q * 2 + c) * U, U), U)
            thl[0, rows, :] = hi
            thl[1, rows, :] = lo

    def tile(rows, q):
        cols = pl.ds(pl.multiple_of(q * 2 * U, 2 * U), 2 * U)
        xh, xl = xhl[0, rows, :], xhl[1, rows, :]
        th, tl = thl[0, cols, :], thl[1, cols, :]
        lg[rows, cols] = scale * (dot_nt(xh, th) + dot_nt(xh, tl) + dot_nt(xl, th))

    def unit_rows(a):
        return pl.ds(pl.multiple_of(a * U, U), U)

    def block(pose_slots, text_slots):
        pa = [pabs(*s) for s in pose_slots]
        qa = [qabs(*s) for s in text_slots]

        def body(i):
            a = pick(i // len(qa), pa)
            tile(unit_rows(a), pick(i % len(qa), qa))

        loop(len(pa) * len(qa), body)

    for kind in range(2):
        got(kind, (0, 3), 0)
        send(kind, (0, 3), 0, NXT, (0, 2))
        got(kind, (1, 0), 0)
        send(kind, (1, 0), 0, NXT, (1, 3))
        send(kind, (1, 0), 0, PRV, (1, 1))
        got(kind, (0, 1), 0)
    convert_pose((0, 0))
    for kind in range(2):
        got(kind, (0, 1), 1)
        send(kind, (0, 1), 1, PRV, (0, 2))
        got(kind, (1, 0), 1)
        send(kind, (1, 0), 1, NXT, (1, 3))
        send(kind, (1, 0), 1, PRV, (1, 1))
        got(kind, (0, 3), 1)
    near = [(0, 0), (0, 3), (0, 1), (1, 0)]
    for s in near[1:]:
        convert_pose(s)
    for s in near:
        got_sib(s)
        convert_text(s)
    block(near, near)
    far = (0, 2)
    for kind in range(2):
        for h in range(2):
            got(kind, far, h)
            send(kind, far, h, PAR, (1, 2))
    convert_pose(far)
    got_sib(far)
    convert_text(far)
    block([far], near + [far])
    block(near, [far])
    last = [(1, 3), (1, 1), (1, 2)]
    for s in last:
        for kind in range(2):
            for h in range(2):
                got(kind, s, h)
        convert_pose(s)
    block(last, near + [far])
    for s in last:
        got_sib(s)
        convert_text(s)
    qs = [qabs(*s) for s in last]

    def all_rows(i):
        tile(pl.ds(pl.multiple_of((i // 3) * 256, 256), 256), pick(i % 3, qs))

    loop(12, all_rows)

    nt = 2 * 8

    def row_stats(a):
        rows = unit_rows(a)
        top = lg[rows, 0:U]
        for j in range(1, nt):
            top = jnp.maximum(top, lg[rows, j * U : (j + 1) * U])
        m = jnp.max(top, axis=1, keepdims=True)
        acc = jnp.exp(lg[rows, 0:U] - m)
        for j in range(1, nt):
            acc = acc + jnp.exp(lg[rows, j * U : (j + 1) * U] - m)
        mt = jnp.max(top.T, axis=0, keepdims=True)
        st = jnp.sum(acc.T, axis=0, keepdims=True)
        rowst[pl.ds(a, 1), :] = mt + jnp.log(st)

    loop(8, row_stats)

    def col_stats(b):
        cols = unit_rows(b)
        v = lg[:, cols]
        m = jnp.max(v, axis=0, keepdims=True)
        s = jnp.sum(jnp.exp(v - m), axis=0, keepdims=True)
        colst[pl.ds(b, 1), :] = m + jnp.log(s)

    loop(nt, col_stats)

    for n, d in enumerate(pose_peers):
        copy(rowst, rowrec.at[me_p], row_send.at[n], row_recv.at[(-d[0]) % 2 * 4 + (-d[1]) % 4], pose_peer(*d))
    for n, d in enumerate(text_peers):
        copy(
            colst,
            colrec.at[me_q],
            col_send.at[n],
            col_recv.at[((-d[0]) % 2 * 4 + (-d[1]) % 4) * 2 + d[2]],
            text_peer(*d),
        )
    rowrec[me_p] = rowst[...]
    colrec[me_q] = colst[...]
    for d in pose_peers:
        await_recv(posbuf.at[pabs(*d)], pos_recv.at[d[0] * 4 + d[1]])
    for d in pose_peers:
        await_recv(rowrec.at[pabs(*d)], row_recv.at[d[0] * 4 + d[1]])
    for d in text_peers:
        a = qabs(d[0], d[1]) * 2 + (core + d[2]) % 2
        await_recv(colrec.at[a], col_recv.at[(d[0] * 4 + d[1]) * 2 + d[2]])

    def lse_of(ref, n):
        m = ref[0]
        for j in range(1, n):
            m = jnp.maximum(m, ref[j])
        s = jnp.exp(ref[0] - m)
        for j in range(1, n):
            s = s + jnp.exp(ref[j] - m)
        return m + jnp.log(s)

    row_lse = lse_of(rowrec, 8)
    col_lse = lse_of(colrec, 16)
    rowst2 = rowrec.at[8]
    colst2 = colrec.at[16]
    rowst2[...] = row_lse
    colst2[...] = col_lse

    macc[...] = jnp.zeros_like(macc)

    def slope(a):
        rows = unit_rows(a)
        rl = jnp.broadcast_to(rowst2[pl.ds(a, 1), :], (U, U)).T
        ids = jnp.broadcast_to(posbuf[a][0:1, :].astype(F32), (U, U)).T
        lane = lax.broadcasted_iota(jnp.int32, (1, U), 1)
        acc = jnp.zeros((U, U), F32)
        for j in range(nt):
            cols = slice(j * U, (j + 1) * U)
            v = lg[rows, cols]
            cl = colst2[j : j + 1, :]
            yh = j // 8
            tt = (yhi + ylo + yh) % 2 * 4 + x
            base = (j * 8 + tt) * U
            hit = ids == (base + lane).astype(F32)
            p = 0.5 * (jnp.exp(v - rl) + jnp.exp(v - cl))
            acc = acc + jnp.where(hit, v, 0.0)
            hi, lo = split(jnp.where(hit, p - 1.0, p))
            s_hi[rows, cols] = hi
            s_lo[rows, cols] = lo
        t = acc[0:8]
        for k in range(1, U // 8):
            t = t + acc[k * 8 : (k + 1) * 8]
        macc[...] += t

    loop(8, slope)

    own = 0.5 * (rowst2[pl.ds(me_p, 1), :] + colst2[pl.ds(me_q, 1), :])
    first = lax.broadcasted_iota(jnp.int32, (8, U), 0) == 0
    la[me_p] = jnp.where(first, jnp.broadcast_to(own, (8, U)), 0.0) - macc[...]
    for n, d in enumerate(pose_peers):
        b = la.at[me_p]
        copy(b, b, la_send.at[n], la_recv.at[(-d[0]) % 2 * 4 + (-d[1]) % 4], pose_peer(*d))

    def pose_unit(slot):
        a = pabs(*slot)
        rows = unit_rows(a)
        sh, sl = s_hi[rows, :], s_lo[rows, :]
        gp[a] = dot_nn(sh, thl[0]) + dot_nn(sh, thl[1]) + dot_nn(sl, thl[0])

    def text_pair(slot):
        q = qabs(*slot)
        cols = pl.ds(pl.multiple_of(q * 2 * U, 2 * U), 2 * U)
        sh, sl = s_hi[:, cols], s_lo[:, cols]
        g = dot_nn(xt[0], sh) + dot_nn(xt[0], sl) + dot_nn(xt[1], sh)
        gt[q * 2] = g[:, 0:U]
        gt[q * 2 + 1] = g[:, U : 2 * U]
        i = slot[0] * 4 + slot[1]
        copy(gt.at[q * 2 + 1 - core], rsib.at[i], rsib_send.at[i], rsib_recv.at[i], text_peer(0, 0, 1))

    def g_at(kind, slot):
        if kind == 0:
            return gp.at[pabs(*slot)]
        return gt.at[qabs(*slot) * 2 + core]

    def r_at(kind, i):
        return (rp if kind == 0 else rt).at[i]

    def half(ref, h):
        n = ref.shape[0] // 2
        return ref.at[pl.ds(h * n, n)]

    rs_count = [0, 0]
    def rs_send_to(kind, slot, h, to, i):
        n = rs_count[kind]
        rs_count[kind] += 1
        copy(
            half(g_at(kind, slot), h),
            half(r_at(kind, i), h),
            rs_send.at[kind, n],
            rs_recv.at[kind, i * 2 + h],
            peer(kind, *to),
        )

    def rs_add(kind, slot, i, h):
        await_recv(half(r_at(kind, i), h), rs_recv.at[kind, i * 2 + h])
        dst, src = half(g_at(kind, slot), h), half(r_at(kind, i), h)
        dst[...] += src[...]

    def sib_add(slot):
        i = slot[0] * 4 + slot[1]
        await_recv(rsib.at[i], rsib_recv.at[i])
        dst = g_at(1, slot)
        dst[...] += rsib[i]

    def stage_a(kind):
        for h in range(2):
            rs_send_to(kind, (1, 2), h, PAR, 0)

    def stage_b(kind):
        for h in range(2):
            rs_send_to(kind, (1, 1), h, NXT, 1)
            rs_send_to(kind, (1, 3), h, PRV, 2)

    def stage_c(kind):
        rs_add(kind, (0, 2), 0, 0)
        rs_send_to(kind, (0, 2), 0, PRV, 3)
        rs_add(kind, (0, 2), 0, 1)
        rs_send_to(kind, (0, 2), 1, NXT, 3)

    def stage_d(kind):
        for h in range(2):
            rs_add(kind, (1, 0), 1, h)
            rs_add(kind, (1, 0), 2, h)
            rs_send_to(kind, (1, 0), h, PAR, 4)

    def stage_e(kind):
        rs_send_to(kind, (0, 3), 1, PRV, 5)
        rs_send_to(kind, (0, 1), 0, NXT, 6)
        rs_add(kind, (0, 3), 3, 0)
        rs_send_to(kind, (0, 3), 0, PRV, 5)
        rs_add(kind, (0, 1), 3, 1)
        rs_send_to(kind, (0, 1), 1, NXT, 6)

    pose_unit((1, 2))
    stage_a(0)
    text_pair((1, 2))
    pose_unit((1, 1))
    pose_unit((1, 3))
    stage_b(0)
    sib_add((1, 2))
    stage_a(1)
    text_pair((1, 1))
    text_pair((1, 3))
    pose_unit((0, 2))
    stage_c(0)
    sib_add((1, 1))
    sib_add((1, 3))
    stage_b(1)

    for d in pose_peers:
        await_recv(la.at[pabs(*d)], la_recv.at[d[0] * 4 + d[1]])
    t = la[0]
    for j in range(1, 8):
        t = t + la[j]
    lb[me_q] = t
    for n, d in enumerate(text_peers):
        b = lb.at[me_q]
        copy(
            b,
            b,
            lb_send.at[n],
            lb_recv.at[((-d[0]) % 2 * 4 + (-d[1]) % 4) * 2 + d[2]],
            text_peer(*d),
        )

    text_pair((0, 2))
    pose_unit((1, 0))
    stage_d(0)
    sib_add((0, 2))
    stage_c(1)
    text_pair((1, 0))
    pose_unit((0, 1))
    pose_unit((0, 3))
    stage_e(0)
    sib_add((1, 0))
    stage_d(1)
    text_pair((0, 1))
    text_pair((0, 3))
    pose_unit((0, 0))
    sib_add((0, 1))
    sib_add((0, 3))
    stage_e(1)
    text_pair((0, 0))
    sib_add((0, 0))

    for d in text_peers:
        a = qabs(d[0], d[1]) * 2 + (core + d[2]) % 2
        await_recv(lb.at[a], lb_recv.at[(d[0] * 4 + d[1]) * 2 + d[2]])
    t = lb[0]
    for j in range(1, 16):
        t = t + lb[j]
    loss_ref[0, 0] = jnp.sum(t) / total

    for h in range(2):
        for i in (4, 5, 6):
            rs_add(0, (0, 0), i, h)
    pg_ref[...] = scale * gp[me_p]
    for h in range(2):
        for i in (4, 5, 6):
            rs_add(1, (0, 0), i, h)
    tg_ref[...] = (scale * gt[me_q]).T

    for c in pending:
        c.wait_send()


def per_device(pose_emb, text_emb, positive):
    rows, width = pose_emb.shape
    total = rows * lax.axis_size("pose") * lax.axis_size("text")
    scale = 2.0 / math.sqrt(width)
    dma = pltpu.SemaphoreType.DMA
    vmem = pltpu.VMEM
    full = pl.BlockSpec(memory_space=pltpu.VMEM)
    loss, pose_grad, text_grad = pl.pallas_call(
        functools.partial(kernel, scale, total),
        out_shape=(
            jax.ShapeDtypeStruct((1, 1), F32),
            jax.ShapeDtypeStruct((rows, width), F32),
            jax.ShapeDtypeStruct((rows, width), F32),
        ),
        in_specs=[full] * 3,
        out_specs=(pl.BlockSpec(memory_space=pltpu.SMEM), full, full),
        scratch_shapes=[
            vmem((8, U, width), F32),
            vmem((16, U, width), F32),
            vmem((2, 8 * U, width), BF16),
            vmem((2, width, 8 * U), BF16),
            vmem((2, 16 * U, width), BF16),
            vmem((8 * U, 16 * U), F32),
            vmem((8 * U, 16 * U), BF16),
            vmem((8 * U, 16 * U), BF16),
            vmem((8, U, width), F32),
            vmem((16, width, U), F32),
            vmem((7, U, width), F32),
            vmem((7, width, U), F32),
            vmem((8, width, U), F32),
            vmem((8, 8, U), jnp.int32),
            vmem((8, U), F32),
            vmem((16, U), F32),
            vmem((9, 8, U), F32),
            vmem((17, 16, U), F32),
            vmem((8, 8, U), F32),
            vmem((16, 8, U), F32),
            vmem((8, U), F32),
            dma((2, 16)),
            dma((2, 16)),
            dma((16,)),
            dma((16,)),
            dma((8,)),
            dma((8,)),
            dma((8,)),
            dma((8,)),
            dma((16,)),
            dma((16,)),
            dma((8,)),
            dma((8,)),
            dma((16,)),
            dma((16,)),
            dma((2, 16)),
            dma((2, 16)),
            dma((8,)),
            dma((8,)),
        ],
        compiler_params=pltpu.CompilerParams(
            collective_id=0, has_side_effects=True, vmem_limit_bytes=64 * 1024 * 1024 - 64 * 1024
        ),
    )(pose_emb, text_emb, positive.reshape(1, rows))
    return (loss.reshape(()), pose_grad, text_grad)


def solution(mesh):
    return jax.shard_map(
        per_device,
        mesh=mesh,
        in_specs=(P(("pose", "text"), None), P(("pose", "text"), None), P(("pose", "text"))),
        out_specs=(P(), P(("pose", "text"), None), P(("pose", "text"), None)),
        check_vma=False,
    )
```

time: 526 us -> 129 us (0.25)
  blocking collectives: 184 us -> 0 us
  waiting for transfers between devices: 165 us -> 0 us
  matrix products: 126 us -> 0 us
  Pallas kernels: 0 us -> 124 us
  between operations: 16.9 us -> 2.41 us
  local copies, waits for them, and re-layouts: 16.9 us -> 2.57 us
  other arithmetic: 8.91 us -> 0 us
  loops' own time: 8.15 us -> 0 us
    dot_general x16 -> x0, matrix products: 126 us -> none  [the longest x8 65.6 us: logit_block(): jnp.dot(rows, cols.T, precision=lax.Precision.HIGHEST, preferred_element_...]
    pallas_call x0 -> x1, Pallas kernels: none -> 124 us  [per_device(): pl.pallas_call(functools.partial(kernel, scale, total), out_shape=(jax.Sh...]
    all_gather x5 -> x0, blocking collectives: 113 us -> none  [the longest x4 96.8 us: combined_all(): gathered = jax.tree.map(lambda a: lax.all_gather(a, axis), part)]
    all_gather x2 -> x0, waiting for transfers between devices: 98.8 us -> none  [the longest x1 69.6 us: per_device(): text_blk = lax.all_gather(text_emb, 'pose', axis=0, tiled=True)]
    psum x1 -> x0, blocking collectives: 71.1 us -> none  [per_device(): loss = lax.psum(share, ('pose', 'text')) / total]
    reduce_scatter x2 -> x0, waiting for transfers between devices: 64.1 us -> none  [the longest x1 64.1 us: per_device(): lax.psum_scatter(text_part, 'pose', scatter_dimension=0, tiled=True)]
    while x28 -> x0, local copies, waits for them, and re-layouts: 10.6 us -> none
    another operation x4 -> x0, loops' own time: 8.15 us -> none  [the longest x1 4.62 us: block_stats(): lax.scan(block_one, init, jnp.arange(rows_all // step, dtype=jnp.int32))]
  transfers between devices with their start and end apart: 4 -> 0, of which waited for: 3 -> 0; matrix products, arithmetic and copies ran while one was open for 0% -> 0% of each run, Pallas kernels for 0% -> 0%
where the time goes in v1:
time: 129 us
  Pallas kernels  124 us (96%)
  local copies, waits for them, and re-layouts  2.57 us (2%)
  between operations  2.41 us (2%)
    pallas_call x1, Pallas kernels, per_device(): pl.pallas_call(functools.partial(kernel, scale, total), out_shape=(jax.Sh...  124 us

profile of v1, /device:TPU:1, one launch (start us, length us, event | category | flops | bytes accessed | tf_op | source)
XLA Modules:
  0.0 128.7 jit_solution(17875071161455208744)
XLA Ops:
  0.6 123.7 %shard_map.58 = (f32[1,1]{1,0:T(1,128)}, f32[128,768]{1,0:T(8,128)}, f32[128,768]{1,0:T(8,128)}) custom-call(f32[128,768]{1,0:T(8,128)} %pose_ref.1, f32[128,768]{1,0:T(8,128)} %text_ref.1, s32[1,128]{1,0:T(1,128)} %bitcast.2), custom_call_target="tpu_custom_call" | custom-call | tf_op jit(solution)/shard_map/pallas_call | solution.py:542
  125.0 0.0 copy-start
  125.0 1.8 %copy.10 = f32[128,768]{1,0:T(8,128)} copy(f32[128,768]{1,0:T(8,128)} %get-tuple-element.13) | data formatting | bytes 786432
  126.8 0.0 copy-done
  126.8 0.7 copy.11
Async XLA Ops:
  125.0 1.8 %copy-start = (f32[128,768]{1,0:T(8,128)S(1)}, f32[128,768]{1,0:T(8,128)}, u32[]{:S(2)}) copy-start(f32[128,768]{1,0:T(8,128)} %get-tuple-element.14) | copy-start | bytes 1179652
